TPU v7x, 32 devices: a whole 2x2x4 slice. The times are simulated.
32 devices in a mesh: front: 4 (over z), row: 4 (over x, core), col: 2 (over y).
Axes of the slice: x: 2, y: 2, z: 4, core: 2. Of those that a mesh axis runs over, the one named last changes fastest.
Arguments:
- sigma_anc: bfloat16 [8192, 8192], P(('front', 'row'), 'col'), may hold values from -6 to 6
- update_blocks: int32 [4, 32], replicated, may hold values from 0 to 63, as said below
- panel: bfloat16 [4, 4096, 2048], P('front', 'col'), may hold values from -0.09375 to 0.09375
Outputs:
- sigma_ju: bfloat16 [4, 2048, 4096], P('front', 'col', 'row')
Inputs may be any that keep to these rules, and one draw needn't show every extreme that they name: `update_blocks`: A front's update blocks are 32 distinct blocks in increasing order along the row. Each class of blocks g, (g // 4) mod (4), holds exactly 8 of them, and each aligned run of 32 blocks holds exactly 16 of them.
All inputs are finite; a program needn't handle non-finite values.
Results may differ from a plain program's by a relative error of at most 0.017.
Values may be sent and summed in bfloat16 or wider, within the bound.
A program may use at most 64 MiB of HBM per device.

v0:
```python
import jax
import jax.numpy as jnp
from jax import lax
from jax.sharding import PartitionSpec as P

BLK = 128
NANC = 4
SEPB = 16
UB = 32


def on_device(sigma_anc, update_blocks, panel):
    front_count = lax.axis_size("front")
    row_count = lax.axis_size("row")
    col_count = lax.axis_size("col")
    blocks_total = NANC * SEPB
    range_blocks = blocks_total // (front_count * row_count)
    octant_blocks = blocks_total // col_count
    class_picks = UB // row_count
    octant_picks = UB // col_count
    my_front = lax.axis_index("front")
    my_row = lax.axis_index("row")
    my_col = lax.axis_index("col")
    own_list = lax.dynamic_index_in_dim(update_blocks, my_front, 0, keepdims=False)
    classes = own_list // range_blocks % row_count
    ranking = jnp.argsort(classes * UB + jnp.arange(UB, dtype=jnp.int32))
    class_rank = lax.dynamic_slice_in_dim(ranking, my_row * class_picks, class_picks)
    class_blocks = jnp.take(own_list, class_rank)
    source_front = class_blocks // (range_blocks * row_count)
    source_slot = class_blocks % range_blocks
    strips = sigma_anc.reshape(range_blocks, BLK, octant_blocks, BLK)
    held_blocks = (my_front * row_count + my_row) * range_blocks + jnp.arange(
        range_blocks, dtype=jnp.int32
    )
    living = jnp.any(update_blocks[:, None, :] == held_blocks[None, :, None], axis=2)
    column_lists = (
        lax.dynamic_slice_in_dim(update_blocks, my_col * octant_picks, octant_picks, 1)
        - my_col * octant_blocks
    )

    def select_columns(column_ids):
        return jnp.take(strips, column_ids, axis=2)

    selected = jax.vmap(select_columns)(column_lists)
    outgoing = jnp.where(living[:, :, None, None, None], selected, jnp.zeros((), selected.dtype))
    arrived = lax.all_to_all(outgoing, "front", split_axis=0, concat_axis=0, tiled=True)
    flat_arrived = arrived.reshape(front_count * range_blocks, BLK, octant_picks, BLK)
    gathered = jnp.take(flat_arrived, source_front * range_blocks + source_slot, axis=0)
    square = gathered.reshape(class_picks * BLK, octant_picks * BLK)
    panel_rows = panel[0]
    summed = lax.psum_scatter(
        lax.dot_general(
            panel_rows, square, (((0,), (1,)), ((), ())), preferred_element_type=jnp.float32
        ).astype(jnp.bfloat16),
        "col",
        scatter_dimension=0,
        tiled=True,
    ).astype(jnp.float32)
    return (-summed).astype(jnp.bfloat16)[None]


def solution(mesh):
    placed = (P(("front", "row"), "col"), P(), P("front", "col", None))
    return jax.shard_map(
        on_device, mesh=mesh, in_specs=placed, out_specs=P("front", "col", "row"), check_vma=False
    )
```

profile of v0, /device:TPU:0, one launch (start us, length us, event | category | flops | bytes accessed | tf_op | source)
XLA Modules:
  0.0 310.9 jit_solution(11740143850295797394)
XLA Ops:
  6.5 3.4 %copy.13 = bf16[64,8,32,128]{3,2,1,0:T(8,128)(2,1)S(1)} copy(bf16[64,8,32,128]{3,1,2,0:T(8,128)(2,1)} %bitcast.28) | data formatting | bytes 8388608
  10.0 0.0 copy-start
  10.0 3.6 %copy.10 = bf16[4,128,32,128]{3,1,2,0:T(8,128)(2,1)} copy(bf16[4,128,32,128]{3,2,1,0:T(8,128)(2,1)S(1)} %bitcast.27) | data formatting | bytes 8388608 | tf_op jit(solution)/shard_map/reshape | solution.py:31
  13.6 0.0 copy-done
  13.6 0.1 compare_and_fusion
  13.7 0.1 reshape.104
  13.8 0.2 compare_reduce_fusion
  14.0 7.7 %gather_fusion.1 = bf16[64,4,128,128]{3,2,1,0:T(8,128)(2,1)} fusion(bf16[4,128,32,128]{3,1,2,0:T(8,128)(2,1)} %copy.10, s32[1024]{0:T(1024)S(1)} %pad_clamp_fusion.1), kind=kCustom, calls=%fused_computation.1 | custom fusion | bytes 16777472 | tf_op jit(solution)/shard_map/vmap(jit(_take))/gather | solution.py:42
  21.7 12.0 %fusion.3 = bf16[4,4,128,16,128]{4,3,2,1,0:T(8,128)(2,1)} fusion(bf16[4,16,4,128,128]{4,3,2,1,0:T(8,128)(2,1)} %bitcast.26, pred[4,4]{1,0:T(4,128)(4,1)S(1)} %compare_reduce_fusion, pred[4,16]{1,0:T(4,128)(4,1)S(1)} %get-tuple-element.11), kind=kLoop, calls=%fused_computation.7 | loop fusion | flops 8388608 | bytes 16777296 | tf_op jit(solution)/shard_map/jit(_where)/select_n | solution.py:45
  33.7 6.3 %all-to-all-start = ((bf16[4,4,128,16,128]{4,3,2,1,0:T(8,128)(2,1)}), bf16[4,4,128,16,128]{4,3,2,1,0:T(8,128)(2,1)}, u32[]{:S(2)}, u32[]{:S(2)}) async-start(bf16[4,4,128,16,128]{4,3,2,1,0:T(8,128)(2,1)} %fusion.3), calls=%async_computation | async-start | bytes 16777216 | tf_op jit(solution)/shard_map/all_to_all | solution.py:46
  40.0 0.0 reduce-scatter.2.cloned.1.call-start
  40.0 1.6 sort.17
  41.6 0.1 compare_select_fusion.2
  41.7 0.6 gather_fusion
  42.4 0.1 compare_and_fusion.1
  42.5 181.6 %all-to-all-done = bf16[4,4,128,16,128]{4,3,2,1,0:T(8,128)(2,1)} async-done(((bf16[4,4,128,16,128]{4,3,2,1,0:T(8,128)(2,1)}), bf16[4,4,128,16,128]{4,3,2,1,0:T(8,128)(2,1)}, u32[]{:S(2)}, u32[]{:S(2)}) %all-to-all-start) | async-done | bytes 8388640 | tf_op jit(solution)/shard_map/all_to_all | solution.py:46
  224.1 6.4 %gather_fusion.2 = bf16[8,128,16,128]{3,2,1,0:T(8,128)(2,1)} fusion(bf16[16,128,16,128]{3,2,1,0:T(8,128)(2,1)} %bitcast.3, s32[1024]{0:T(1024)S(1)} %pad_clamp_fusion), kind=kCustom, calls=%fused_computation.2 | custom fusion | bytes 8388640 | tf_op jit(solution)/shard_map/jit(_take)/gather | solution.py:48
  230.5 2.7 broadcast_select_fusion
  233.2 12.6 %convert_bitcast_fusion = bf16[2048,1024]{0,1:T(8,128)(2,1)} fusion(bf16[1,2048,2048]{2,1,0:T(8,128)(2,1)} %param.5, bf16[128,8,16,128]{3,2,1,0:T(8,128)(2,1)S(1)} %bitcast.29), kind=kOutput, calls=%fused_computation.11 | convolution fusion | flops 8592031744 | bytes 16777216 | tf_op jit(solution)/shard_map/dot_general | solution.py:52
  245.7 0.0 reduce-scatter.2.cloned.1.call-update
  245.8 53.6 %reduce-scatter.2.cloned.1.call-done = bf16[1024,1024]{0,1:T(8,128)(2,1)} async-done(((bf16[2048,1024]{0,1:T(8,128)(2,1)}), bf16[1024,1024]{0,1:T(8,128)(2,1)}) %reduce-scatter.2.cloned.1.call-update) | async-done | bytes 2097168 | tf_op jit(solution)/shard_map/reduce_scatter | solution.py:51
  299.4 2.1 fusion.10
  301.5 2.6 copy.12
  (6 shorter events, 0.0 us)
Async XLA Ops:
  10.0 3.6 %copy-start = (s32[4,32]{1,0:T(4,128)S(1)}, s32[4,32]{1,0:T(4,128)}, u32[]{:S(2)}) copy-start(s32[4,32]{1,0:T(4,128)} %param.4) | copy-start | bytes 1540
  33.7 190.4 %all-to-all-start = ((bf16[4,4,128,16,128]{4,3,2,1,0:T(8,128)(2,1)}), bf16[4,4,128,16,128]{4,3,2,1,0:T(8,128)(2,1)}, u32[]{:S(2)}, u32[]{:S(2)}) async-start(bf16[4,4,128,16,128]{4,3,2,1,0:T(8,128)(2,1)} %fusion.3), calls=%async_computation | async-start | bytes 16777216 | tf_op jit(solution)/shard_map/all_to_all | solution.py:46
  40.0 259.4 %reduce-scatter.2.cloned.1.call-start = ((), (), s32[]{:S(2)}) async-start(), calls=%async_computation.2 | async-start | bytes 6291456 | tf_op jit(solution)/shard_map/reduce_scatter | solution.py:51
Sparse Core Ops, SparseCore 0:
  245.9 53.4 reduce-scatter.1
where the time goes:
time: 311 us
  waiting for transfers between devices  235 us (76%)
  local copies, waits for them, and re-layouts  24.5 us (8%)
  other arithmetic  18.8 us (6%)
  between operations  13.4 us (4%)
  matrix products  12.6 us (4%)
  starting transfers between devices  6.32 us (2%)
    all_to_all x1, waiting for transfers between devices, on_device(): lax.all_to_all(outgoing, 'front', split_axis=0, concat_axis=0, tiled=True)  182 us
    reduce_scatter x1, waiting for transfers between devices, on_device(): lax.psum_scatter(lax.dot_general(panel_rows, square, (((0,), (1,)), ((),...  53.6 us
    dot_general x1, matrix products, on_device(): lax.dot_general(panel_rows, square, (((0,), (1,)), ((), ())), preferred_e...  12.6 us
    select_n x1, other arithmetic, on_device(): jnp.where(living[:, :, None, None, None], selected, jnp.zeros((), selecte...  12 us
    gather x1, local copies, waits for them, and re-layouts, select_columns(): return jnp.take(strips, column_ids, axis=2)  7.71 us
    gather x1, local copies, waits for them, and re-layouts, on_device(): jnp.take(flat_arrived, source_front * range_blocks + source_slot, axis=0)  6.44 us
    all_to_all x1, starting transfers between devices, on_device(): lax.all_to_all(outgoing, 'front', split_axis=0, concat_axis=0, tiled=True)  6.32 us
  transfers between devices with their start and end apart: 2, of which 2 were waited for; matrix products, arithmetic and copies ran while one was open for 1% of the time, Pallas kernels for 0%

commit v1 on v0

v1 whole, which is shorter than its diff:
```python
import functools

import jax
import jax.numpy as jnp
from jax import lax
from jax.experimental import pallas as pl
from jax.experimental.pallas import tpu as pltpu
from jax.sharding import PartitionSpec as P

BLK = 128
NANC = 4
SEPB = 16
UB = 32
MESH = pl.DeviceIdType.MESH


def flipped(index, mask, count):
    total, bit = 0, 1
    while bit < count:
        digit = lax.rem(lax.div(index, bit), 2)
        total = total + (1 - digit if mask & bit else digit) * bit
        bit *= 2
    return total


def kernel(
    fronts, rows, cols,
    chosen_ref, panel_ref, result,
    panel, inbox, part, landed,
    own_sem, panel_sem, send_sem, recv_sem, part_send, part_recv,
):
    my_front = lax.axis_index("front")
    my_col = lax.axis_index("col")
    slots = chosen_ref.shape[1]
    wide = panel_ref.shape[1]
    share = wide // cols
    tile = min(512, share)
    per_share = share // tile
    masks = list(range(fronts - 1, 0, -1))

    def own_copy(slot):
        return pltpu.make_async_copy(
            chosen_ref.at[my_front, slot], inbox.at[0, slot], own_sem.at[slot]
        )

    panel_copy = pltpu.make_async_copy(panel_ref, panel, panel_sem)

    barrier = pltpu.get_barrier_semaphore()
    for mask in masks:
        pl.semaphore_signal(
            barrier, inc=1, device_id={"front": flipped(my_front, mask, fronts)}, device_id_type=MESH
        )
    for step in range(1, cols):
        pl.semaphore_signal(
            barrier, inc=1, device_id={"col": lax.rem(my_col + step, cols)}, device_id_type=MESH
        )
    pl.semaphore_wait(barrier, fronts - 1 + cols - 1)

    def front_copy(mask, slot):
        return pltpu.make_async_remote_copy(
            src_ref=chosen_ref.at[flipped(my_front, mask, fronts), slot],
            dst_ref=inbox.at[mask, slot],
            send_sem=send_sem.at[mask - 1, slot],
            recv_sem=recv_sem.at[mask - 1, slot],
            device_id={"front": flipped(my_front, mask, fronts)},
            device_id_type=MESH,
        )

    def dispatch(slot, carry):
        for mask in masks:
            front_copy(mask, slot).start()
        return carry

    lax.fori_loop(0, slots, dispatch, 0)
    for slot in range(slots):
        own_copy(slot).start()
    panel_copy.start()
    for slot in range(slots):
        own_copy(slot).wait()
    panel_copy.wait()

    def part_copy(mask, slot, step):
        return pltpu.make_async_remote_copy(
            src_ref=part.at[mask, slot, lax.rem(my_col + step, cols)],
            dst_ref=landed.at[mask, slot, step - 1],
            send_sem=part_send.at[mask, slot, step - 1],
            recv_sem=part_recv.at[mask, slot, step - 1],
            device_id={"col": lax.rem(my_col + step, cols)},
            device_id_type=MESH,
        )

    def multiply(mask, slot):
        def one_tile(n, carry):
            lanes = pl.ds(pl.multiple_of(n * tile, tile), tile)
            inner = pl.ds(pl.multiple_of(lax.rem(n, per_share) * tile, tile), tile)
            product = jnp.dot(inbox[mask, slot], panel[:, lanes], preferred_element_type=jnp.float32)
            part[mask, slot, lax.div(n, per_share), :, inner] = product.astype(part.dtype)
            return carry

        lax.fori_loop(0, wide // tile, one_tile, 0)
        for step in range(1, cols):
            part_copy(mask, slot, step).start()

    def finish(mask, slot):
        for step in range(1, cols):
            part_copy(mask, slot, step).wait_recv()
        place = flipped(my_front, mask, fronts) * slots + slot
        width = min(256, share)
        for at in range(0, share, width):
            total = part[mask, slot, my_col, :, at:at + width].astype(jnp.float32)
            for step in range(1, cols):
                total = total + landed[mask, slot, step - 1, :, at:at + width].astype(jnp.float32)
            result[place, at:at + width, :] = (-total).T.astype(result.dtype)

    def own_product(slot, carry):
        multiply(0, slot)
        return carry

    lax.fori_loop(0, slots, own_product, 0)

    def own_finish(slot, carry):
        finish(0, slot)
        return carry

    lax.fori_loop(0, slots, own_finish, 0)

    def arrival(slot, carry):
        for mask in range(1, fronts):
            front_copy(mask, slot).wait_recv()
            multiply(mask, slot)
            if mask > 1:
                finish(mask - 1, slot)
            else:
                @pl.when(slot > 0)
                def _():
                    finish(fronts - 1, slot - 1)
        return carry

    lax.fori_loop(0, slots, arrival, 0)

    finish(fronts - 1, slots - 1)

    def drain(slot, carry):
        for mask in range(fronts):
            if mask > 0:
                front_copy(mask, slot).wait_send()
            for step in range(1, cols):
                part_copy(mask, slot, step).wait_send()
        return carry

    lax.fori_loop(0, slots, drain, 0)


def choose(cols, ids_ref, sigma_ref, chosen_ref):
    my_col = lax.axis_index("col")
    octant_blocks = NANC * SEPB // cols
    picks = UB // cols
    for front in range(chosen_ref.shape[0]):
        for j in range(picks):
            column = ids_ref[front, my_col * picks + j] - my_col * octant_blocks
            lanes = pl.ds(pl.multiple_of(column * BLK, BLK), BLK)
            chosen_ref[front, 0, :, j * BLK:(j + 1) * BLK] = sigma_ref[:, lanes]


def arrange(slots, rows, ids_ref, result_ref, out_ref):
    my_front = lax.axis_index("front")
    my_row = lax.axis_index("row")
    class_picks = UB // rows
    count = jnp.int32(0)
    places = [jnp.int32(0)] * class_picks
    for i in range(UB):
        block = ids_ref[my_front, i]
        hit = lax.rem(lax.div(block, slots), rows) == my_row
        place = lax.div(block, slots * rows) * slots + lax.rem(block, slots)
        for k in range(min(class_picks, i + 1)):
            places[k] = jnp.where(jnp.logical_and(hit, count == k), place, places[k])
        count = count + jnp.where(hit, 1, 0)
    for k, place in enumerate(places):
        out_ref[:, k * BLK:(k + 1) * BLK] = result_ref[place]


def solution(mesh):
    fronts, rows, cols = mesh.shape["front"], mesh.shape["row"], mesh.shape["col"]

    def on_device(sigma_anc, update_blocks, panel):
        depth, wide = panel.shape[1:]
        share = wide // cols
        slots = sigma_anc.shape[0] // BLK
        kind = sigma_anc.dtype
        smem = pl.BlockSpec(memory_space=pltpu.SMEM)
        vmem = pl.BlockSpec(memory_space=pltpu.VMEM)
        hbm = pl.BlockSpec(memory_space=pl.ANY)
        chosen = pl.pallas_call(
            functools.partial(choose, cols),
            grid=(slots,),
            out_shape=jax.ShapeDtypeStruct((fronts, slots, BLK, depth), kind),
            in_specs=[smem, pl.BlockSpec((BLK, sigma_anc.shape[1]), lambda slot: (slot, 0))],
            out_specs=pl.BlockSpec((fronts, 1, BLK, depth), lambda slot: (0, slot, 0, 0)),
            compiler_params=pltpu.CompilerParams(vmem_limit_bytes=32 * 1024 * 1024),
        )(update_blocks, sigma_anc)
        result = pl.pallas_call(
            functools.partial(kernel, fronts, rows, cols),
            out_shape=jax.ShapeDtypeStruct((fronts * slots, share, BLK), kind),
            in_specs=[hbm, hbm],
            out_specs=vmem,
            scratch_shapes=[
                pltpu.VMEM((depth, wide), kind),
                pltpu.VMEM((fronts, slots, BLK, depth), kind),
                pltpu.VMEM((fronts, slots, cols, BLK, share), kind),
                pltpu.VMEM((fronts, slots, cols - 1, BLK, share), kind),
                pltpu.SemaphoreType.DMA((slots,)),
                pltpu.SemaphoreType.DMA,
                pltpu.SemaphoreType.DMA((fronts - 1, slots)),
                pltpu.SemaphoreType.DMA((fronts - 1, slots)),
                pltpu.SemaphoreType.DMA((fronts, slots, cols - 1)),
                pltpu.SemaphoreType.DMA((fronts, slots, cols - 1)),
            ],
            compiler_params=pltpu.CompilerParams(
                collective_id=0, has_side_effects=True, vmem_limit_bytes=56 * 1024 * 1024
            ),
            cost_estimate=pl.CostEstimate(
                flops=2 * fronts * slots * BLK * depth * wide,
                bytes_accessed=2 * (sigma_anc.size + panel[0].size),
                transcendentals=0,
            ),
        )(chosen, panel[0])
        product = pl.pallas_call(
            functools.partial(arrange, slots, rows),
            out_shape=jax.ShapeDtypeStruct((share, UB // rows * BLK), kind),
            in_specs=[smem, vmem],
            out_specs=vmem,
            compiler_params=pltpu.CompilerParams(vmem_limit_bytes=32 * 1024 * 1024),
        )(update_blocks, result)
        return product[None]

    placed = (P(("front", "row"), "col"), P(), P("front", "col", None))
    return jax.shard_map(
        on_device, mesh=mesh, in_specs=placed, out_specs=P("front", "col", "row"), check_vma=False
    )
```

time: 311 us -> 219 us (0.70)
  waiting for transfers between devices: 235 us -> 0 us
  Pallas kernels: 0 us -> 211 us
  other arithmetic: 18.8 us -> 0 us
  local copies, waits for them, and re-layouts: 24.5 us -> 8.26 us
  between operations: 13.4 us -> 0.04 us
  matrix products: 12.6 us -> 0 us
  starting transfers between devices: 6.32 us -> 0 us
    pallas_call x0 -> x3, Pallas kernels: none -> 211 us  [the longest x1 204 us: on_device(): pl.pallas_call(functools.partial(kernel, fronts, rows, cols), out_shape=j...]
    all_to_all x1 -> x0, waiting for transfers between devices: 182 us -> none  [on_device(): lax.all_to_all(outgoing, 'front', split_axis=0, concat_axis=0, tiled=True)]
    reduce_scatter x1 -> x0, waiting for transfers between devices: 53.6 us -> none  [on_device(): lax.psum_scatter(lax.dot_general(panel_rows, square, (((0,), (1,)), ((),...]
    gather x3 -> x0, local copies, waits for them, and re-layouts: 14.8 us -> none  [the longest x1 7.71 us: select_columns(): return jnp.take(strips, column_ids, axis=2)]
    select_n x3 -> x0, other arithmetic: 14.7 us -> none  [the longest x1 12 us: on_device(): jnp.where(living[:, :, None, None, None], selected, jnp.zeros((), selecte...]
    dot_general x1 -> x0, matrix products: 12.6 us -> none  [on_device(): lax.dot_general(panel_rows, square, (((0,), (1,)), ((), ())), preferred_e...]
    all_to_all x1 -> x0, starting transfers between devices: 6.32 us -> none  [on_device(): lax.all_to_all(outgoing, 'front', split_axis=0, concat_axis=0, tiled=True)]
    unnamed x3 -> x10, local copies, waits for them, and re-layouts: 3.44 us -> 8.26 us
  transfers between devices with their start and end apart: 2 -> 0, of which waited for: 2 -> 0; matrix products, arithmetic and copies ran while one was open for 1% -> 0% of each run, Pallas kernels for 0% -> 0%
where the time goes in v1:
time: 219 us
  Pallas kernels  211 us (96%)
  local copies, waits for them, and re-layouts  8.26 us (4%)
    pallas_call x1, Pallas kernels, on_device(): pl.pallas_call(functools.partial(kernel, fronts, rows, cols), out_shape=j...  204 us
    unnamed x10, local copies, waits for them, and re-layouts  8.26 us

profile of v1, /device:TPU:0, one launch (start us, length us, event | category | flops | bytes accessed | tf_op | source)
XLA Modules:
  0.0 218.9 jit_solution(7210480628253798332)
XLA Ops:
  0.0 0.0 copy-start.1
  0.0 2.2 copy-done.1
  2.2 0.0 copy-start.3
  2.2 0.7 copy-done.3
  2.9 3.5 %shard_map.37.chosen_ref = bf16[4,4,128,2048]{3,2,1,0:T(8,128)(2,1)S(1)} custom-call(s32[4,32]{1,0:T(4,128)S(1)} %copy-done.3, bf16[512,4096]{1,0:T(8,128)(2,1)S(1)} %copy-done.1), custom_call_target="tpu_custom_call" | custom-call | tf_op jit(solution)/shard_map/pallas_call | solution.py:193
  6.4 0.0 copy-start
  6.4 3.2 %copy-done = bf16[4,4,128,2048]{3,2,1,0:T(8,128)(2,1)} copy-done((bf16[4,4,128,2048]{3,2,1,0:T(8,128)(2,1)}, bf16[4,4,128,2048]{3,2,1,0:T(8,128)(2,1)S(1)}, u32[]{:S(2)}) %copy-start) | copy-done | bytes 8388632
  9.6 0.0 copy-start.4
  9.6 204.1 %shard_map.38.result_ref = bf16[16,1024,128]{2,1,0:T(8,128)(2,1)} custom-call(bf16[4,4,128,2048]{3,2,1,0:T(8,128)(2,1)} %copy-done, bf16[2048,2048]{1,0:T(8,128)(2,1)} %bitcast.2), custom_call_target="tpu_custom_call" | custom-call | flops 17179869184 | bytes 12582912 | tf_op jit(solution)/shard_map/pallas_call | solution.py:201
  213.7 0.0 copy-done.4
  213.7 0.0 copy-start.2
  213.7 2.2 copy-done.2
  215.9 3.0 %shard_map.39 = bf16[1024,1024]{1,0:T(8,128)(2,1)} custom-call(s32[4,32]{1,0:T(4,128)S(1)} %copy-done.4, bf16[16,1024,128]{2,1,0:T(8,128)(2,1)S(1)} %copy-done.2), custom_call_target="tpu_custom_call" | custom-call | tf_op jit(solution)/shard_map/pallas_call | solution.py:227
Async XLA Ops:
  0.0 2.2 copy-start.1
  2.2 0.7 copy-start.3
  6.4 3.2 %copy-start = (bf16[4,4,128,2048]{3,2,1,0:T(8,128)(2,1)}, bf16[4,4,128,2048]{3,2,1,0:T(8,128)(2,1)S(1)}, u32[]{:S(2)}) copy-start(bf16[4,4,128,2048]{3,2,1,0:T(8,128)(2,1)S(1)} %shard_map.37.chosen_ref) | copy-start | bytes 25165828
  9.6 204.1 %copy-start.4 = (s32[4,32]{1,0:T(4,128)S(1)}, s32[4,32]{1,0:T(4,128)}, u32[]{:S(2)}) copy-start(s32[4,32]{1,0:T(4,128)} %ids_ref.3) | copy-start | bytes 1540
  213.7 2.2 copy-start.2

commit v2 on v1

v2 whole, which is shorter than its diff:
```python
import functools

import jax
import jax.numpy as jnp
from jax import lax
from jax.experimental import pallas as pl
from jax.experimental.pallas import tpu as pltpu
from jax.sharding import PartitionSpec as P

BLK = 128
NANC = 4
SEPB = 16
UB = 32
MESH = pl.DeviceIdType.MESH


def flipped(index, mask, count):
    total, bit = 0, 1
    while bit < count:
        digit = lax.rem(lax.div(index, bit), 2)
        total = total + (1 - digit if mask & bit else digit) * bit
        bit *= 2
    return total


def deal(fronts, rows, sigma_ref, dealt_ref, own_sem, send_sem, recv_sem):
    my_front = lax.axis_index("front")
    my_row = lax.axis_index("row")
    strip = BLK // (2 * rows)
    side = lax.rem(my_front, 2)
    place = side * rows + my_row

    def strips(to_side, to_row):
        return sigma_ref.at[:, pl.ds(pl.multiple_of((to_row * 2 + to_side) * strip, strip), strip)]

    moves = [(flip, step) for flip in (1, 0) for step in range(rows) if flip or step]

    def target(flip, step):
        return {
            "front": flipped(my_front, flip, fronts),
            "row": lax.rem(my_row + step, rows),
        }

    own = pltpu.make_async_copy(strips(side, my_row), dealt_ref.at[place], own_sem)
    own.start()
    barrier = pltpu.get_barrier_semaphore()
    for flip, step in moves:
        pl.semaphore_signal(barrier, inc=1, device_id=target(flip, step), device_id_type=MESH)
    pl.semaphore_wait(barrier, len(moves))
    copies = []
    for flip, step in moves:
        to_side = 1 - side if flip else side
        copies.append(
            pltpu.make_async_remote_copy(
                src_ref=strips(to_side, lax.rem(my_row + step, rows)),
                dst_ref=dealt_ref.at[place],
                send_sem=send_sem.at[flip, step],
                recv_sem=recv_sem.at[flip, step],
                device_id=target(flip, step),
                device_id_type=MESH,
            )
        )
    for copy in copies:
        copy.start()
    own.wait()
    for copy in copies:
        copy.wait()


def choose(cols, ids_ref, dealt_ref, chosen_ref):
    front = pl.program_id(0)
    octant = lax.div(lax.axis_index("front"), 2)
    my_col = lax.axis_index("col")
    octant_blocks = NANC * SEPB // cols
    picks = UB // cols
    pieces = chosen_ref.shape[1]
    strip = dealt_ref.shape[1]
    each = picks // pieces
    lanes = []
    for j in range(picks):
        column = ids_ref[front, my_col * picks + j] - my_col * octant_blocks
        lanes.append(pl.ds(pl.multiple_of(column * BLK, BLK), BLK))
    for p in range(picks):
        block = ids_ref[front, octant * picks + p] - octant * octant_blocks
        at = p % each * strip
        for j in range(picks):
            chosen_ref[0, p // each, at:at + strip, j * BLK:(j + 1) * BLK] = dealt_ref[block, :, lanes[j]]


def kernel(
    fronts, rows, cols,
    chosen_ref, panel_ref, result,
    panel, inbox, part, landed,
    own_sem, panel_sem, send_sem, recv_sem, part_send, part_recv, row_send, row_recv,
):
    my_front = lax.axis_index("front")
    my_row = lax.axis_index("row")
    my_col = lax.axis_index("col")
    pieces = chosen_ref.shape[1]
    strip = BLK // (2 * rows)
    picks = UB // cols
    each = picks // pieces
    wide = panel_ref.shape[1]
    share = wide // cols
    tile = min(512, share)
    per_share = share // tile
    masks = list(range(fronts - 1, 0, -1))

    def own_copy(piece):
        return pltpu.make_async_copy(
            chosen_ref.at[my_front, piece], inbox.at[0, piece], own_sem.at[piece]
        )

    panel_copy = pltpu.make_async_copy(panel_ref, panel, panel_sem)

    barrier = pltpu.get_barrier_semaphore()
    for mask in masks:
        pl.semaphore_signal(
            barrier, inc=1, device_id={"front": flipped(my_front, mask, fronts)}, device_id_type=MESH
        )
    for step in range(1, cols):
        pl.semaphore_signal(
            barrier, inc=1, device_id={"col": lax.rem(my_col + step, cols)}, device_id_type=MESH
        )
    for step in range(1, rows):
        pl.semaphore_signal(
            barrier, inc=1, device_id={"row": lax.rem(my_row + step, rows)}, device_id_type=MESH
        )
    pl.semaphore_wait(barrier, fronts + cols + rows - 3)

    def front_copy(mask, piece):
        return pltpu.make_async_remote_copy(
            src_ref=chosen_ref.at[flipped(my_front, mask, fronts), piece],
            dst_ref=inbox.at[mask, piece],
            send_sem=send_sem.at[mask - 1, piece],
            recv_sem=recv_sem.at[mask - 1, piece],
            device_id={"front": flipped(my_front, mask, fronts)},
            device_id_type=MESH,
        )

    def dispatch(piece, carry):
        for mask in masks:
            front_copy(mask, piece).start()
        return carry

    lax.fori_loop(0, pieces, dispatch, 0)
    for piece in range(pieces):
        own_copy(piece).start()
    panel_copy.start()
    for piece in range(pieces):
        own_copy(piece).wait()
    panel_copy.wait()

    def part_copy(mask, piece, step):
        return pltpu.make_async_remote_copy(
            src_ref=part.at[mask, piece, lax.rem(my_col + step, cols)],
            dst_ref=landed.at[mask, piece, step - 1],
            send_sem=part_send.at[mask, piece, step - 1],
            recv_sem=part_recv.at[mask, piece, step - 1],
            device_id={"col": lax.rem(my_col + step, cols)},
            device_id_type=MESH,
        )

    def spot(mask, piece):
        source = flipped(my_front, mask, fronts)
        first = lax.div(source, 2) * picks + piece * each
        offset = (my_row * 2 + lax.rem(source, 2)) * strip
        return first, pl.ds(pl.multiple_of(offset, strip), strip)

    def row_copy(mask, piece, step):
        first, lines = spot(mask, piece)
        return pltpu.make_async_remote_copy(
            src_ref=result.at[pl.ds(first, each), lines],
            dst_ref=result.at[pl.ds(first, each), lines],
            send_sem=row_send.at[mask, piece, step - 1],
            recv_sem=row_recv.at[mask, piece, step - 1],
            device_id={"row": lax.rem(my_row + step, rows)},
            device_id_type=MESH,
        )

    def multiply(mask, piece):
        def one_tile(n, carry):
            lanes = pl.ds(pl.multiple_of(n * tile, tile), tile)
            inner = pl.ds(pl.multiple_of(lax.rem(n, per_share) * tile, tile), tile)
            product = jnp.dot(inbox[mask, piece], panel[:, lanes], preferred_element_type=jnp.float32)
            part[mask, piece, lax.div(n, per_share), :, inner] = product.astype(part.dtype)
            return carry

        lax.fori_loop(0, wide // tile, one_tile, 0)
        for step in range(1, cols):
            part_copy(mask, piece, step).start()

    def finish(mask, piece):
        for step in range(1, cols):
            part_copy(mask, piece, step).wait_recv()
        first, lines = spot(mask, piece)
        for p in range(each):
            inside = slice(p * strip, (p + 1) * strip)
            total = part[mask, piece, my_col, inside, :].astype(jnp.float32)
            for step in range(1, cols):
                total = total + landed[mask, piece, step - 1, inside, :].astype(jnp.float32)
            result[first + p, lines, :] = (-total).astype(result.dtype)
        for step in range(1, rows):
            row_copy(mask, piece, step).start()

    for mask in (0, 1):
        def product_of(piece, carry, mask=mask):
            if mask:
                front_copy(mask, piece).wait_recv()
            multiply(mask, piece)
            return carry

        def total_of(piece, carry, mask=mask):
            finish(mask, piece)
            return carry

        lax.fori_loop(0, pieces, product_of, 0)
        lax.fori_loop(0, pieces, total_of, 0)

    def arrival(piece, carry):
        for mask in range(2, fronts):
            front_copy(mask, piece).wait_recv()
            multiply(mask, piece)
            if mask > 2:
                finish(mask - 1, piece)
            else:
                @pl.when(piece > 0)
                def _():
                    finish(fronts - 1, piece - 1)
        return carry

    lax.fori_loop(0, pieces, arrival, 0)
    finish(fronts - 1, pieces - 1)

    def drain(piece, carry):
        for mask in range(fronts):
            if mask > 0:
                front_copy(mask, piece).wait_send()
            for step in range(1, cols):
                part_copy(mask, piece, step).wait_send()
            for step in range(1, rows):
                row_copy(mask, piece, step).wait()
        return carry

    lax.fori_loop(0, pieces, drain, 0)


def arrange(slots, rows, ids_ref, result_ref, out_ref):
    my_front = lax.axis_index("front")
    my_row = lax.axis_index("row")
    class_picks = UB // rows
    count = jnp.int32(0)
    places = [jnp.int32(0)] * class_picks
    for i in range(UB):
        hit = lax.rem(lax.div(ids_ref[my_front, i], slots), rows) == my_row
        for k in range(min(class_picks, i + 1)):
            places[k] = jnp.where(jnp.logical_and(hit, count == k), i, places[k])
        count = count + jnp.where(hit, 1, 0)
    for k, place in enumerate(places):
        out_ref[:, k * BLK:(k + 1) * BLK] = result_ref[place].T


def solution(mesh):
    fronts, rows, cols = mesh.shape["front"], mesh.shape["row"], mesh.shape["col"]

    def on_device(sigma_anc, update_blocks, panel):
        depth, wide = panel.shape[1:]
        share = wide // cols
        slots = sigma_anc.shape[0] // BLK
        across = sigma_anc.shape[1]
        kind = sigma_anc.dtype
        strip = BLK // (2 * rows)
        picks = UB // cols
        pieces = min(4, picks)
        lines = picks // pieces * strip
        smem = pl.BlockSpec(memory_space=pltpu.SMEM)
        vmem = pl.BlockSpec(memory_space=pltpu.VMEM)
        hbm = pl.BlockSpec(memory_space=pl.ANY)
        mib = 1024 * 1024
        dealt = pl.pallas_call(
            functools.partial(deal, fronts, rows),
            out_shape=jax.ShapeDtypeStruct((2 * rows, slots, strip, across), kind),
            in_specs=[hbm],
            out_specs=hbm,
            scratch_shapes=[
                pltpu.SemaphoreType.DMA,
                pltpu.SemaphoreType.DMA((2, rows)),
                pltpu.SemaphoreType.DMA((2, rows)),
            ],
            compiler_params=pltpu.CompilerParams(
                collective_id=1, has_side_effects=True, vmem_limit_bytes=56 * mib
            ),
        )(sigma_anc.reshape(slots, BLK, across))
        chosen = pl.pallas_call(
            functools.partial(choose, cols),
            grid=(fronts,),
            out_shape=jax.ShapeDtypeStruct((fronts, pieces, lines, depth), kind),
            in_specs=[smem, vmem],
            out_specs=pl.BlockSpec((1, pieces, lines, depth), lambda front: (front, 0, 0, 0)),
            compiler_params=pltpu.CompilerParams(vmem_limit_bytes=56 * mib),
        )(update_blocks, dealt.reshape(2 * rows * slots, strip, across))
        result = pl.pallas_call(
            functools.partial(kernel, fronts, rows, cols),
            out_shape=jax.ShapeDtypeStruct((UB, BLK, share), kind),
            in_specs=[hbm, hbm],
            out_specs=vmem,
            scratch_shapes=[
                pltpu.VMEM((depth, wide), kind),
                pltpu.VMEM((fronts, pieces, lines, depth), kind),
                pltpu.VMEM((fronts, pieces, cols, lines, share), kind),
                pltpu.VMEM((fronts, pieces, cols - 1, lines, share), kind),
                pltpu.SemaphoreType.DMA((pieces,)),
                pltpu.SemaphoreType.DMA,
                pltpu.SemaphoreType.DMA((fronts - 1, pieces)),
                pltpu.SemaphoreType.DMA((fronts - 1, pieces)),
                pltpu.SemaphoreType.DMA((fronts, pieces, cols - 1)),
                pltpu.SemaphoreType.DMA((fronts, pieces, cols - 1)),
                pltpu.SemaphoreType.DMA((fronts, pieces, rows - 1)),
                pltpu.SemaphoreType.DMA((fronts, pieces, rows - 1)),
            ],
            compiler_params=pltpu.CompilerParams(
                collective_id=0, has_side_effects=True, vmem_limit_bytes=56 * mib
            ),
            cost_estimate=pl.CostEstimate(
                flops=2 * fronts * pieces * lines * depth * wide,
                bytes_accessed=2 * (sigma_anc.size + panel[0].size),
                transcendentals=0,
            ),
        )(chosen, panel[0])
        product = pl.pallas_call(
            functools.partial(arrange, slots, rows),
            out_shape=jax.ShapeDtypeStruct((share, UB // rows * BLK), kind),
            in_specs=[smem, vmem],
            out_specs=vmem,
            compiler_params=pltpu.CompilerParams(vmem_limit_bytes=56 * mib),
        )(update_blocks, result)
        return product[None]

    placed = (P(("front", "row"), "col"), P(), P("front", "col", None))
    return jax.shard_map(
        on_device, mesh=mesh, in_specs=placed, out_specs=P("front", "col", "row"), check_vma=False
    )
```

time: 219 us -> 209 us (0.954)
  the two profiles are of different devices: /device:TPU:0 before, /device:TPU:9 now
where the time goes in v2:
time: 209 us
  Pallas kernels  209 us (100%)
    pallas_call x1, Pallas kernels, on_device(): pl.pallas_call(functools.partial(kernel, fronts, rows, cols), out_shape=j...  149 us
    pallas_call x1, Pallas kernels, on_device(): pl.pallas_call(functools.partial(deal, fronts, rows), out_shape=jax.Shape...  49.4 us
    pallas_call x1, Pallas kernels, on_device(): pl.pallas_call(functools.partial(arrange, slots, rows), out_shape=jax.Sha...  5.62 us
    pallas_call x1, Pallas kernels, on_device(): pl.pallas_call(functools.partial(choose, cols), grid=(fronts,), out_shape...  5.38 us

profile of v2, /device:TPU:9, one launch (start us, length us, event | category | flops | bytes accessed | tf_op | source)
XLA Modules:
  0.0 208.9 jit_solution(1436252801191264813)
XLA Ops:
  0.0 49.4 %shard_map.37 = bf16[8,4,16,4096]{3,2,1,0:T(8,128)(2,1)} custom-call(bf16[4,128,4096]{2,1,0:T(8,128)(2,1)} %bitcast.5), custom_call_target="tpu_custom_call" | custom-call | tf_op jit(solution)/shard_map/pallas_call | solution.py:280
  49.4 5.4 %shard_map.38.chosen_ref = bf16[4,4,64,2048]{3,2,1,0:T(8,128)(2,1)} custom-call(s32[4,32]{1,0:T(4,128)} %ids_ref.3, bf16[32,16,4096]{2,1,0:T(8,128)(2,1)} %bitcast.4), custom_call_target="tpu_custom_call" | custom-call | tf_op jit(solution)/shard_map/pallas_call | solution.py:294
  54.8 148.5 %shard_map.39.result_ref = bf16[32,128,1024]{2,1,0:T(8,128)(2,1)} custom-call(bf16[4,4,64,2048]{3,2,1,0:T(8,128)(2,1)} %shard_map.38.chosen_ref, bf16[2048,2048]{1,0:T(8,128)(2,1)} %bitcast.6), custom_call_target="tpu_custom_call" | custom-call | flops 8589934592 | bytes 12582912 | tf_op jit(solution)/shard_map/pallas_call | solution.py:302
  203.3 5.6 %shard_map.40 = bf16[1024,1024]{1,0:T(8,128)(2,1)} custom-call(s32[4,32]{1,0:T(4,128)} %ids_ref.3, bf16[32,128,1024]{2,1,0:T(8,128)(2,1)} %shard_map.39.result_ref), custom_call_target="tpu_custom_call" | custom-call | tf_op jit(solution)/shard_map/pallas_call | solution.py:330

commit v3 on v2

--- a/solution.py
+++ b/solution.py
@@ -105,6 +105,7 @@
     tile = min(512, share)
     per_share = share // tile
     masks = list(range(fronts - 1, 0, -1))
+    order = masks[::-1]
 
     def own_copy(piece):
         return pltpu.make_async_copy(
@@ -203,34 +204,31 @@
         for step in range(1, rows):
             row_copy(mask, piece, step).start()
 
-    for mask in (0, 1):
-        def product_of(piece, carry, mask=mask):
-            if mask:
-                front_copy(mask, piece).wait_recv()
-            multiply(mask, piece)
-            return carry
-
-        def total_of(piece, carry, mask=mask):
-            finish(mask, piece)
-            return carry
-
-        lax.fori_loop(0, pieces, product_of, 0)
-        lax.fori_loop(0, pieces, total_of, 0)
+    def own_product(piece, carry):
+        multiply(0, piece)
+        return carry
+
+    def own_total(piece, carry):
+        finish(0, piece)
+        return carry
+
+    lax.fori_loop(0, pieces, own_product, 0)
+    lax.fori_loop(0, pieces, own_total, 0)
 
     def arrival(piece, carry):
-        for mask in range(2, fronts):
+        for at, mask in enumerate(order):
             front_copy(mask, piece).wait_recv()
             multiply(mask, piece)
-            if mask > 2:
-                finish(mask - 1, piece)
+            if at:
+                finish(order[at - 1], piece)
             else:
                 @pl.when(piece > 0)
                 def _():
-                    finish(fronts - 1, piece - 1)
+                    finish(order[-1], piece - 1)
         return carry
 
     lax.fori_loop(0, pieces, arrival, 0)
-    finish(fronts - 1, pieces - 1)
+    finish(order[-1], pieces - 1)
 
     def drain(piece, carry):
         for mask in range(fronts):

time: 209 us -> 193 us (0.923)
  the two profiles are of different devices: /device:TPU:9 before, /device:TPU:0 now
where the time goes in v3:
time: 193 us; the launch traced here: 191 us
  Pallas kernels  191 us (99%)
    pallas_call x1, Pallas kernels, on_device(): pl.pallas_call(functools.partial(kernel, fronts, rows, cols), out_shape=j...  130 us
    pallas_call x1, Pallas kernels, on_device(): pl.pallas_call(functools.partial(deal, fronts, rows), out_shape=jax.Shape...  50.5 us
    pallas_call x1, Pallas kernels, on_device(): pl.pallas_call(functools.partial(arrange, slots, rows), out_shape=jax.Sha...  5.62 us
    pallas_call x1, Pallas kernels, on_device(): pl.pallas_call(functools.partial(choose, cols), grid=(fronts,), out_shape...  5.38 us

profile of v3, /device:TPU:0, one launch (start us, length us, event | category | flops | bytes accessed | tf_op | source)
XLA Modules:
  0.0 191.2 jit_solution(13672843792162506300)
XLA Ops:
  0.0 50.5 %shard_map.37 = bf16[8,4,16,4096]{3,2,1,0:T(8,128)(2,1)} custom-call(bf16[4,128,4096]{2,1,0:T(8,128)(2,1)} %bitcast.5), custom_call_target="tpu_custom_call" | custom-call | tf_op jit(solution)/shard_map/pallas_call | solution.py:278
  50.5 5.4 %shard_map.38.chosen_ref = bf16[4,4,64,2048]{3,2,1,0:T(8,128)(2,1)} custom-call(s32[4,32]{1,0:T(4,128)} %ids_ref.3, bf16[32,16,4096]{2,1,0:T(8,128)(2,1)} %bitcast.4), custom_call_target="tpu_custom_call" | custom-call | tf_op jit(solution)/shard_map/pallas_call | solution.py:292
  55.9 129.7 %shard_map.39.result_ref = bf16[32,128,1024]{2,1,0:T(8,128)(2,1)} custom-call(bf16[4,4,64,2048]{3,2,1,0:T(8,128)(2,1)} %shard_map.38.chosen_ref, bf16[2048,2048]{1,0:T(8,128)(2,1)} %bitcast.6), custom_call_target="tpu_custom_call" | custom-call | flops 8589934592 | bytes 12582912 | tf_op jit(solution)/shard_map/pallas_call | solution.py:300
  185.6 5.6 %shard_map.40 = bf16[1024,1024]{1,0:T(8,128)(2,1)} custom-call(s32[4,32]{1,0:T(4,128)} %ids_ref.3, bf16[32,128,1024]{2,1,0:T(8,128)(2,1)} %shard_map.39.result_ref), custom_call_target="tpu_custom_call" | custom-call | tf_op jit(solution)/shard_map/pallas_call | solution.py:328

commit v4 on v3

--- a/solution.py
+++ b/solution.py
@@ -162,22 +162,26 @@
             device_id_type=MESH,
         )
 
-    def spot(mask, piece):
+    def spot(mask, piece, row):
         source = flipped(my_front, mask, fronts)
         first = lax.div(source, 2) * picks + piece * each
-        offset = (my_row * 2 + lax.rem(source, 2)) * strip
+        offset = (row * 2 + lax.rem(source, 2)) * strip
         return first, pl.ds(pl.multiple_of(offset, strip), strip)
 
-    def row_copy(mask, piece, step):
-        first, lines = spot(mask, piece)
+    def row_copy(mask, piece, kind):
+        first, lines = spot(mask, piece, flipped(my_row, 2, rows) if kind == 2 else my_row)
         return pltpu.make_async_remote_copy(
             src_ref=result.at[pl.ds(first, each), lines],
             dst_ref=result.at[pl.ds(first, each), lines],
-            send_sem=row_send.at[mask, piece, step - 1],
-            recv_sem=row_recv.at[mask, piece, step - 1],
-            device_id={"row": lax.rem(my_row + step, rows)},
+            send_sem=row_send.at[mask, piece, kind],
+            recv_sem=row_recv.at[mask, piece, kind],
+            device_id={"row": flipped(my_row, 1 if kind else 2, rows)},
             device_id_type=MESH,
         )
+
+    def relay(mask, piece):
+        row_copy(mask, piece, 0).wait_recv()
+        row_copy(mask, piece, 2).start()
 
     def multiply(mask, piece):
         def one_tile(n, carry):
@@ -194,15 +198,15 @@
     def finish(mask, piece):
         for step in range(1, cols):
             part_copy(mask, piece, step).wait_recv()
-        first, lines = spot(mask, piece)
+        first, lines = spot(mask, piece, my_row)
         for p in range(each):
             inside = slice(p * strip, (p + 1) * strip)
             total = part[mask, piece, my_col, inside, :].astype(jnp.float32)
             for step in range(1, cols):
                 total = total + landed[mask, piece, step - 1, inside, :].astype(jnp.float32)
             result[first + p, lines, :] = (-total).astype(result.dtype)
-        for step in range(1, rows):
-            row_copy(mask, piece, step).start()
+        row_copy(mask, piece, 0).start()
+        row_copy(mask, piece, 1).start()
 
     def own_product(piece, carry):
         multiply(0, piece)
@@ -214,21 +218,30 @@
 
     lax.fori_loop(0, pieces, own_product, 0)
     lax.fori_loop(0, pieces, own_total, 0)
+
+    def own_relay(piece, carry):
+        relay(0, piece)
+        return carry
+
+    lax.fori_loop(0, pieces, own_relay, 0)
 
     def arrival(piece, carry):
         for at, mask in enumerate(order):
             front_copy(mask, piece).wait_recv()
             multiply(mask, piece)
-            if at:
-                finish(order[at - 1], piece)
-            else:
-                @pl.when(piece > 0)
-                def _():
-                    finish(order[-1], piece - 1)
+            for lag, action in ((1, finish), (2, relay)):
+                if at >= lag:
+                    action(order[at - lag], piece)
+                else:
+                    @pl.when(piece > 0)
+                    def _(action=action, earlier=order[at - lag]):
+                        action(earlier, piece - 1)
         return carry
 
     lax.fori_loop(0, pieces, arrival, 0)
     finish(order[-1], pieces - 1)
+    relay(order[-2], pieces - 1)
+    relay(order[-1], pieces - 1)
 
     def drain(piece, carry):
         for mask in range(fronts):
@@ -236,8 +249,9 @@
                 front_copy(mask, piece).wait_send()
             for step in range(1, cols):
                 part_copy(mask, piece, step).wait_send()
-            for step in range(1, rows):
-                row_copy(mask, piece, step).wait()
+            row_copy(mask, piece, 0).wait_send()
+            row_copy(mask, piece, 1).wait()
+            row_copy(mask, piece, 2).wait()
         return carry
 
     lax.fori_loop(0, pieces, drain, 0)

time: 193 us -> 177 us (0.917)
  Pallas kernels: 191 us -> 177 us
    pallas_call x1, Pallas kernels: 130 us -> 115 us  [on_device(): pl.pallas_call(functools.partial(kernel, fronts, rows, cols), out_shape=j...]
where the time goes in v4:
time: 177 us
  Pallas kernels  177 us (100%)
    pallas_call x1, Pallas kernels, on_device(): pl.pallas_call(functools.partial(kernel, fronts, rows, cols), out_shape=j...  115 us
    pallas_call x1, Pallas kernels, on_device(): pl.pallas_call(functools.partial(deal, fronts, rows), out_shape=jax.Shape...  50.5 us
    pallas_call x1, Pallas kernels, on_device(): pl.pallas_call(functools.partial(arrange, slots, rows), out_shape=jax.Sha...  5.62 us
    pallas_call x1, Pallas kernels, on_device(): pl.pallas_call(functools.partial(choose, cols), grid=(fronts,), out_shape...  5.38 us

profile of v4, /device:TPU:0, one launch (start us, length us, event | category | flops | bytes accessed | tf_op | source)
XLA Modules:
  0.0 176.7 jit_solution(8191439389042933631)
XLA Ops:
  0.0 50.5 %shard_map.37 = bf16[8,4,16,4096]{3,2,1,0:T(8,128)(2,1)} custom-call(bf16[4,128,4096]{2,1,0:T(8,128)(2,1)} %bitcast.5), custom_call_target="tpu_custom_call" | custom-call | tf_op jit(solution)/shard_map/pallas_call | solution.py:292
  50.5 5.4 %shard_map.38.chosen_ref = bf16[4,4,64,2048]{3,2,1,0:T(8,128)(2,1)} custom-call(s32[4,32]{1,0:T(4,128)} %ids_ref.3, bf16[32,16,4096]{2,1,0:T(8,128)(2,1)} %bitcast.4), custom_call_target="tpu_custom_call" | custom-call | tf_op jit(solution)/shard_map/pallas_call | solution.py:306
  55.9 115.2 %shard_map.39.result_ref = bf16[32,128,1024]{2,1,0:T(8,128)(2,1)} custom-call(bf16[4,4,64,2048]{3,2,1,0:T(8,128)(2,1)} %shard_map.38.chosen_ref, bf16[2048,2048]{1,0:T(8,128)(2,1)} %bitcast.6), custom_call_target="tpu_custom_call" | custom-call | flops 8589934592 | bytes 12582912 | tf_op jit(solution)/shard_map/pallas_call | solution.py:314
  171.1 5.6 %shard_map.40 = bf16[1024,1024]{1,0:T(8,128)(2,1)} custom-call(s32[4,32]{1,0:T(4,128)} %ids_ref.3, bf16[32,128,1024]{2,1,0:T(8,128)(2,1)} %shard_map.39.result_ref), custom_call_target="tpu_custom_call" | custom-call | tf_op jit(solution)/shard_map/pallas_call | solution.py:342

commit v5 on v4

--- a/solution.py
+++ b/solution.py
@@ -283,7 +283,7 @@
         kind = sigma_anc.dtype
         strip = BLK // (2 * rows)
         picks = UB // cols
-        pieces = min(4, picks)
+        pieces = min(8, picks)
         lines = picks // pieces * strip
         smem = pl.BlockSpec(memory_space=pltpu.SMEM)
         vmem = pl.BlockSpec(memory_space=pltpu.VMEM)

time: 177 us -> 188 us (1.062)
  Pallas kernels: 177 us -> 188 us
    pallas_call x1, Pallas kernels: 115 us -> 127 us  [on_device(): pl.pallas_call(functools.partial(kernel, fronts, rows, cols), out_shape=j...]
where the time goes in v5:
time: 188 us
  Pallas kernels  188 us (100%)
    pallas_call x1, Pallas kernels, on_device(): pl.pallas_call(functools.partial(kernel, fronts, rows, cols), out_shape=j...  127 us
    pallas_call x1, Pallas kernels, on_device(): pl.pallas_call(functools.partial(deal, fronts, rows), out_shape=jax.Shape...  50.5 us
    pallas_call x1, Pallas kernels, on_device(): pl.pallas_call(functools.partial(arrange, slots, rows), out_shape=jax.Sha...  5.62 us
    pallas_call x1, Pallas kernels, on_device(): pl.pallas_call(functools.partial(choose, cols), grid=(fronts,), out_shape...  5.38 us

profile of v5, /device:TPU:0, one launch (start us, length us, event | category | flops | bytes accessed | tf_op | source)
XLA Modules:
  0.0 188.1 jit_solution(12370854475484742085)
XLA Ops:
  0.0 50.5 %shard_map.37 = bf16[8,4,16,4096]{3,2,1,0:T(8,128)(2,1)} custom-call(bf16[4,128,4096]{2,1,0:T(8,128)(2,1)} %bitcast.5), custom_call_target="tpu_custom_call" | custom-call | tf_op jit(solution)/shard_map/pallas_call | solution.py:292
  50.5 5.4 %shard_map.38.chosen_ref = bf16[4,8,32,2048]{3,2,1,0:T(8,128)(2,1)} custom-call(s32[4,32]{1,0:T(4,128)} %ids_ref.3, bf16[32,16,4096]{2,1,0:T(8,128)(2,1)} %bitcast.4), custom_call_target="tpu_custom_call" | custom-call | tf_op jit(solution)/shard_map/pallas_call | solution.py:306
  55.9 126.5 %shard_map.39.result_ref = bf16[32,128,1024]{2,1,0:T(8,128)(2,1)} custom-call(bf16[4,8,32,2048]{3,2,1,0:T(8,128)(2,1)} %shard_map.38.chosen_ref, bf16[2048,2048]{1,0:T(8,128)(2,1)} %bitcast.6), custom_call_target="tpu_custom_call" | custom-call | flops 8589934592 | bytes 12582912 | tf_op jit(solution)/shard_map/pallas_call | solution.py:314
  182.4 5.6 %shard_map.40 = bf16[1024,1024]{1,0:T(8,128)(2,1)} custom-call(s32[4,32]{1,0:T(4,128)} %ids_ref.3, bf16[32,128,1024]{2,1,0:T(8,128)(2,1)} %shard_map.39.result_ref), custom_call_target="tpu_custom_call" | custom-call | tf_op jit(solution)/shard_map/pallas_call | solution.py:342
